TPU v7x, 32 devices: a whole 2x2x4 slice. The times are simulated.
32 devices in a mesh: patch: 4 (over x, core), seq: 8 (over z, y).
Axes of the slice: x: 2, y: 2, z: 4, core: 2. Of those that a mesh axis runs over, the one named last changes fastest.
Arguments:
- fresh_qkv: bfloat16 [3, 576, 192, 128], P(None, ('patch', 'seq')), as said below
- stale_kv: bfloat16 [2, 576, 192, 128], P(None, None, 'seq'), may hold values from -6 to 6
- text_count: int32 [8], replicated, may hold values from 16 to 64
Outputs:
- attended: bfloat16 [576, 192, 128], P(('patch', 'seq'))
- refreshed_kv: bfloat16 [2, 576, 192, 128], P(None, None, 'seq')
Inputs may be any that keep to these rules, and one draw needn't show every extreme that they name: `fresh_qkv`: each entry lies within -100 to 100.
All inputs are finite; a program needn't handle non-finite values.
Results may differ from a plain program's by a relative error of at most 0.0049.
Values may be sent and summed in bfloat16 or wider, within the bound.
A program may use at most 128 MiB of HBM per device.

v0:
```python
import math

import jax
import jax.numpy as jnp
from jax import lax
from jax.sharding import PartitionSpec as P

HEADS = 24
TXT_DEV = 2
IMG_DEV = 16


def attend(query_part, key_part, value_part, valid_counts, text_len):
    score_scale = 1.0 / math.sqrt(query_part.shape[-1])
    position = jnp.arange(key_part.shape[0])

    def per_pair(operands):
        query_rows, key_rows, value_rows, valid_text = operands
        scores = (
            lax.dot_general(
                query_rows, key_rows, (((1,), (1,)), ((), ())), preferred_element_type=jnp.float32
            )
            * score_scale
        )
        visible = (position >= text_len) | (position < valid_text)
        scores = jnp.where(visible[None, :], scores, -jnp.inf)
        highest = jnp.max(scores, axis=1, keepdims=True)
        raised = jnp.exp(scores - highest)
        weights = (raised / jnp.sum(raised, axis=1, keepdims=True)).astype(jnp.bfloat16)
        return jnp.dot(weights, value_rows, preferred_element_type=jnp.float32).astype(jnp.bfloat16)

    outputs = lax.map(
        per_pair,
        (
            jnp.moveaxis(query_part, 1, 0),
            jnp.moveaxis(key_part, 1, 0),
            jnp.moveaxis(value_part, 1, 0),
            valid_counts,
        ),
    )
    return jnp.moveaxis(outputs, 0, 1)


def per_device(fresh_qkv, stale_kv, text_count):
    seq_count = lax.axis_size("seq")
    shard_rows = fresh_qkv.shape[1]
    pairs_here = fresh_qkv.shape[2] // seq_count
    patch_len = shard_rows * seq_count
    patch_index = lax.axis_index("patch")
    first_pair = lax.axis_index("seq") * pairs_here
    exchanged = lax.all_to_all(fresh_qkv, "seq", split_axis=2, concat_axis=1, tiled=True)
    query_part = exchanged[0]
    own_kv = exchanged[1:]
    refreshed = lax.all_gather(own_kv, "patch", axis=1, tiled=True)
    merged_kv = lax.dynamic_update_slice_in_dim(stale_kv, own_kv, patch_index * patch_len, 1)
    seq_len = stale_kv.shape[1]
    text_len = TXT_DEV * seq_len // (TXT_DEV + IMG_DEV)
    image_index = (first_pair + jnp.arange(pairs_here)) // HEADS
    matches = image_index[:, None] == jnp.arange(text_count.shape[0])[None, :]
    valid_counts = jnp.sum(jnp.where(matches, text_count[None, :], 0), axis=1)
    attended_part = attend(query_part, merged_kv[0], merged_kv[1], valid_counts, text_len)
    result = lax.all_to_all(attended_part, "seq", split_axis=0, concat_axis=1, tiled=True)
    return (result, refreshed)


def solution(mesh):
    in_specs = (P(None, ("patch", "seq"), None, None), P(None, None, "seq", None), P())
    out_specs = (P(("patch", "seq"), None, None), P(None, None, "seq", None))
    return jax.shard_map(
        per_device, mesh=mesh, in_specs=in_specs, out_specs=out_specs, check_vma=False
    )
```

profile of v0, /device:TPU:0, one launch (start us, length us, event | category | flops | bytes accessed | tf_op | source)
XLA Modules:
  0.0 259.5 jit_solution(8226788644196565723)
XLA Ops:
  7.2 5.3 %copy.36 = bf16[3,18,192,128]{3,1,0,2:T(8,128)(2,1)} copy(bf16[3,18,192,128]{3,2,1,0:T(8,128)(2,1)} %param.5) | data formatting | bytes 5308416 | tf_op args[0]
  12.5 7.3 %all-to-all-start = ((bf16[3,18,192,128]{3,1,0,2:T(8,128)(2,1)}), bf16[3,18,192,128]{3,1,0,2:T(8,128)(2,1)S(1)}, u32[]{:S(2)}, u32[]{:S(2)}) async-start(bf16[3,18,192,128]{3,1,0,2:T(8,128)(2,1)} %copy.36), calls=%async_computation | async-start | bytes 7077888 | tf_op jit(solution)/shard_map/all_to_all | solution.py:51
  19.8 7.7 %copy.40 = bf16[2,576,24,128]{3,1,2,0:T(8,128)(2,1)} copy(bf16[2,576,24,128]{3,2,1,0:T(8,128)(2,1)} %param.6) | data formatting | bytes 14155776 | tf_op args[1]
  27.6 71.3 %all-to-all-done = bf16[3,18,192,128]{3,1,0,2:T(8,128)(2,1)S(1)} async-done(((bf16[3,18,192,128]{3,1,0,2:T(8,128)(2,1)}), bf16[3,18,192,128]{3,1,0,2:T(8,128)(2,1)S(1)}, u32[]{:S(2)}, u32[]{:S(2)}) %all-to-all-start) | async-done | bytes 2654240 | tf_op jit(solution)/shard_map/all_to_all | solution.py:51
  101.3 1.5 copy.39
  102.8 2.9 %copy_dynamic-update-slice_fusion = bf16[2,576,24,128]{3,1,2,0:T(8,128)(2,1)} fusion(bf16[2,576,24,128]{3,1,2,0:T(8,128)(2,1)} %copy.40, s32[]{:T(128)S(6)} %select_n.22, bf16[2,144,24,128]{3,2,1,0:T(8,128)(2,1)} %bitcast.51), kind=kLoop, calls=%fused_computation.24 | loop fusion | bytes 3538948 | tf_op jit(solution)/shard_map/dynamic_update_slice | solution.py:55
  105.7 5.8 %slice_bitcast_fusion = (bf16[24,576,128]{2,1,0:T(8,128)(2,1)}, bf16[24,576,128]{2,1,0:T(8,128)(2,1)S(1)}) fusion(bf16[2,576,24,128]{3,1,2,0:T(8,128)(2,1)} %copy_dynamic-update-slice_fusion), kind=kLoop, calls=%fused_computation.22 | loop fusion | bytes 14155776 | tf_op jit(solution)/shard_map/transpose | solution.py:37
  111.5 105.5 %while.12 = (s32[]{:T(128)}, bf16[24,144,128]{2,1,0:T(8,128)(2,1)}, s32[24]{0:T(128)S(1)}, bf16[24,144,128]{2,1,0:T(8,128)(2,1)}, bf16[24,576,128]{2,1,0:T(8,128...) while((s32[]{:T(128)}, bf16[24,144,128]{2,1,0:T(8,128)(2,1)}, s32[24]{0:T(128)S(1)}, ...), condition=%wide.region_4.5_spmd.clone.clone, body=%wide.region_1.4_spmd.clone.clone.sunk | while | flops 43150752 | bytes 1370597 | solution.py:32
  112.7 1.1 fusion.25
  114.1 1.8 fusion.27
  118.4 1.8 fusion.27
  121.5 1.1 fusion.25
  122.8 1.8 fusion.27
  125.9 1.1 fusion.25
  127.2 1.8 fusion.27
  130.3 1.1 fusion.25
  131.6 1.8 fusion.27
  136.0 1.8 fusion.27
  139.1 1.1 fusion.25
  140.4 1.8 fusion.27
  144.8 1.8 fusion.27
  149.2 1.8 fusion.27
  152.3 1.1 fusion.25
  153.6 1.8 fusion.27
  156.7 1.1 fusion.25
  158.0 1.8 fusion.27
  162.4 1.8 fusion.27
  165.5 1.1 fusion.25
  166.8 1.8 fusion.27
  171.2 1.8 fusion.27
  174.3 1.1 fusion.25
  175.6 1.8 fusion.27
  180.0 1.8 fusion.27
  183.1 1.1 fusion.25
  184.4 1.8 fusion.27
  188.8 1.8 fusion.27
  191.9 1.1 fusion.25
  193.2 1.8 fusion.27
  197.6 1.8 fusion.27
  200.6 1.1 fusion.25
  202.0 1.8 fusion.27
  206.4 1.8 fusion.27
  210.8 1.8 fusion.27
  215.2 1.8 fusion.27
  217.0 1.4 copy.47
  218.4 26.0 %all_to_all.33 = bf16[144,24,128]{2,1,0:T(8,128)(2,1)S(1)} all-to-all(bf16[144,24,128]{2,1,0:T(8,128)(2,1)S(1)} %bitcast.55), channel_id=1, replica_groups=mesh['patch'=4,'seq'=8] {'seq'}, dimensions={0} | all-to-all | bytes 1769472 | tf_op jit(solution)/shard_map/all_to_all | solution.py:62
  244.4 1.1 copy.44
  245.5 7.2 %copy.59 = bf16[2,576,24,128]{3,2,1,0:T(8,128)(2,1)} copy(bf16[2,576,24,128]{3,2,1,0:T(8,128)(2,1)} %all-gather.2.cloned.1.call-done) | data formatting | bytes 14155776
  (97 shorter events, 50.7 us)
Async XLA Ops:
  12.5 86.4 %all-to-all-start = ((bf16[3,18,192,128]{3,1,0,2:T(8,128)(2,1)}), bf16[3,18,192,128]{3,1,0,2:T(8,128)(2,1)S(1)}, u32[]{:S(2)}, u32[]{:S(2)}) async-start(bf16[3,18,192,128]{3,1,0,2:T(8,128)(2,1)} %copy.36), calls=%async_computation | async-start | bytes 7077888 | tf_op jit(solution)/shard_map/all_to_all | solution.py:51
  19.8 225.7 %all-gather.2.cloned.1.call-start = ((), (), s32[]{:S(2)}) async-start(), calls=%async_computation.2 | async-start | bytes 8847360 | tf_op jit(solution)/shard_map/all_gather | solution.py:54
  19.8 7.7 %copy-start = (s32[8]{0:T(128)S(1)}, s32[8]{0:T(128)}, u32[]{:S(2)}) copy-start(s32[8]{0:T(128)} %param.7) | copy-start | bytes 100
Sparse Core Ops, SparseCore 0:
  102.9 49.8 all-gather.1
where the time goes:
time: 262 us; the launch traced here: 260 us
  waiting for transfers between devices  71.3 us (27%)
  matrix products  70.3 us (27%)
  local copies, waits for them, and re-layouts  49.2 us (19%)
  blocking collectives  26 us (10%)
  other arithmetic  21.2 us (8%)
  between operations  14.1 us (5%)
  starting transfers between devices  7.32 us (3%)
    all_to_all x1, waiting for transfers between devices, per_device(): lax.all_to_all(fresh_qkv, 'seq', split_axis=2, concat_axis=1, tiled=True)  71.3 us
    dot_general x24, matrix products, per_pair(): jnp.dot(weights, value_rows, preferred_element_type=jnp.float32)  43.9 us
    dot_general x24, matrix products, per_pair(): lax.dot_general(query_rows, key_rows, (((1,), (1,)), ((), ())), preferred...  26.4 us
    all_to_all x1, blocking collectives, per_device(): lax.all_to_all(attended_part, 'seq', split_axis=0, concat_axis=1, tiled=T...  26 us
    unnamed x6, local copies, waits for them, and re-layouts  21.3 us
    or x24, other arithmetic, per_pair(): visible = (position >= text_len) | (position < valid_text)  15.6 us
    dynamic_slice x24, local copies, waits for them, and re-layouts, attend(): lax.map(per_pair, (jnp.moveaxis(query_part, 1, 0), jnp.moveaxis(key_part,...  14 us
    all_to_all x1, starting transfers between devices, per_device(): lax.all_to_all(fresh_qkv, 'seq', split_axis=2, concat_axis=1, tiled=True)  7.28 us
  transfers between devices with their start and end apart: 2, of which 1 were waited for; matrix products, arithmetic and copies ran while one was open for 48% of the time, Pallas kernels for 0%

commit v1 on v0

--- a/solution.py
+++ b/solution.py
@@ -1,13 +1,284 @@
+import functools
 import math
 
 import jax
 import jax.numpy as jnp
 from jax import lax
+from jax.experimental import pallas as pl
+from jax.experimental.pallas import tpu as pltpu
 from jax.sharding import PartitionSpec as P
 
 HEADS = 24
 TXT_DEV = 2
 IMG_DEV = 16
+PAIR_TILE = 8
+MESH = pl.DeviceIdType.MESH
+
+
+def fused_kernel(
+    text_len,
+    counts_ref,
+    fresh_ref,
+    stale_ref,
+    attended_ref,
+    refreshed_ref,
+    recv,
+    stale_vmem,
+    wide,
+    keys,
+    values,
+    queries,
+    out_wide,
+    out_send,
+    in_send_sem,
+    in_recv_sem,
+    own_sem,
+    stale_sem,
+    fwd_send_sem,
+    fwd_recv_sem,
+    keep_sem,
+    out_send_sem,
+    out_recv_sem,
+    out_own_sem,
+):
+    _, rows, peers, chunks, tile, hdim = fresh_ref.shape
+    group_len = rows * peers
+    seq_len = stale_ref.shape[1]
+    p = lax.axis_index("patch")
+    s = lax.axis_index("seq")
+    core_twin = p + 1 - 2 * (p % 2)
+    x_twin = (p + 2) % 4
+    scale = 1.0 / math.sqrt(hdim)
+
+    barrier = pltpu.get_barrier_semaphore()
+    for step in range(1, peers):
+        pl.semaphore_signal(
+            barrier, inc=1, device_id=(p, (s + step) % peers), device_id_type=MESH
+        )
+    for twin in (core_twin, x_twin):
+        pl.semaphore_signal(barrier, inc=1, device_id=(twin, s), device_id_type=MESH)
+
+    stale_copies = []
+    for c in range(chunks):
+        for which in range(2):
+            copy = pltpu.make_async_copy(
+                stale_ref.at[which, :, c], stale_vmem.at[which, c], stale_sem.at[which, c]
+            )
+            copy.start()
+            stale_copies.append(copy)
+    own_copies = []
+    for c in range(chunks):
+        copy = pltpu.make_async_copy(
+            fresh_ref.at[:, :, s, c], recv.at[c, :, pl.ds(rows * s, rows)], own_sem.at[c]
+        )
+        copy.start()
+        own_copies.append(copy)
+    pl.semaphore_wait(barrier, peers + 1)
+
+    def in_copy(c, step):
+        to = (s + step) % peers
+        return pltpu.make_async_remote_copy(
+            src_ref=fresh_ref.at[:, :, to, c],
+            dst_ref=recv.at[c, :, pl.ds(rows * s, rows)],
+            send_sem=in_send_sem.at[c, step],
+            recv_sem=in_recv_sem.at[c, step],
+            device_id=(p, to),
+            device_id_type=MESH,
+        )
+
+    def in_arrival(c, step):
+        origin = (s + peers - step) % peers
+        return pltpu.make_async_remote_copy(
+            src_ref=fresh_ref.at[:, :, origin, c],
+            dst_ref=recv.at[c, :, pl.ds(rows * origin, rows)],
+            send_sem=in_send_sem.at[c, step],
+            recv_sem=in_recv_sem.at[c, step],
+            device_id=(p, origin),
+            device_id_type=MESH,
+        )
+
+    def forward(c, kind):
+        if kind == 2:
+            place = refreshed_ref.at[:, pl.ds(group_len * x_twin, group_len), c]
+            source = place
+        else:
+            place = refreshed_ref.at[:, pl.ds(group_len * p, group_len), c]
+            source = recv.at[c, pl.ds(1, 2)]
+        return pltpu.make_async_remote_copy(
+            src_ref=source,
+            dst_ref=place,
+            send_sem=fwd_send_sem.at[kind, c],
+            recv_sem=fwd_recv_sem.at[kind, c],
+            device_id=(x_twin if kind == 0 else core_twin, s),
+            device_id_type=MESH,
+        )
+
+    def forward_arrival(c, kind):
+        origin = {0: x_twin, 1: core_twin, 2: (core_twin + 2) % 4}[kind]
+        return pltpu.make_async_remote_copy(
+            src_ref=recv.at[c, pl.ds(1, 2)],
+            dst_ref=refreshed_ref.at[:, pl.ds(group_len * origin, group_len), c],
+            send_sem=fwd_send_sem.at[kind, c],
+            recv_sem=fwd_recv_sem.at[kind, c],
+            device_id=(x_twin if kind == 0 else core_twin, s),
+            device_id_type=MESH,
+        )
+
+    def keep(c):
+        return pltpu.make_async_copy(
+            recv.at[c, pl.ds(1, 2)],
+            refreshed_ref.at[:, pl.ds(group_len * p, group_len), c],
+            keep_sem.at[c],
+        )
+
+    def out_copy(c, step):
+        to = (s + step) % peers
+        return pltpu.make_async_remote_copy(
+            src_ref=out_send.at[c, pl.ds(rows * to, rows)],
+            dst_ref=attended_ref.at[:, s, c],
+            send_sem=out_send_sem.at[c, step],
+            recv_sem=out_recv_sem.at[c, step],
+            device_id=(p, to),
+            device_id_type=MESH,
+        )
+
+    def out_arrival(c, step):
+        origin = (s + peers - step) % peers
+        return pltpu.make_async_remote_copy(
+            src_ref=out_send.at[c, pl.ds(rows * origin, rows)],
+            dst_ref=attended_ref.at[:, origin, c],
+            send_sem=out_send_sem.at[c, step],
+            recv_sem=out_recv_sem.at[c, step],
+            device_id=(p, origin),
+            device_id_type=MESH,
+        )
+
+    def out_own(c):
+        return pltpu.make_async_copy(
+            out_send.at[c, pl.ds(rows * s, rows)], attended_ref.at[:, s, c], out_own_sem.at[c]
+        )
+
+    for c in range(chunks):
+        for step in range(1, peers):
+            in_copy(c, step).start()
+
+    for copy in stale_copies:
+        copy.wait()
+    for c in range(chunks):
+        for which, target in ((0, keys), (1, values)):
+            wide[...] = stale_vmem[which, c].astype(jnp.float32).reshape(seq_len * tile, hdim)
+            for g in range(tile):
+                target[c * tile + g] = wide[pl.ds(g, seq_len, stride=tile), :].astype(jnp.bfloat16)
+
+    position = lax.broadcasted_iota(jnp.int32, (1, seq_len), 1)
+    for c in range(chunks):
+        own_copies[c].wait()
+        for step in range(1, peers):
+            in_arrival(c, step).wait_recv()
+        forward(c, 0).start()
+        forward(c, 1).start()
+        keep(c).start()
+        for which, target in ((0, queries), (1, keys), (2, values)):
+            part = wide.at[pl.ds(0, group_len * tile)]
+            part[...] = recv[c, which].astype(jnp.float32).reshape(group_len * tile, hdim)
+            for g in range(tile):
+                block = part[pl.ds(g, group_len, stride=tile), :].astype(jnp.bfloat16)
+                if which == 0:
+                    target[g] = block
+                else:
+                    target[c * tile + g, pl.ds(pl.multiple_of(group_len * p, 16), group_len), :] = block
+
+        for g in range(tile):
+            pair = c * tile + g
+            scores = (
+                lax.dot_general(
+                    queries[g],
+                    keys[pair],
+                    (((1,), (1,)), ((), ())),
+                    preferred_element_type=jnp.float32,
+                )
+                * scale
+            )
+            visible = (position >= text_len) | (position < counts_ref[pair])
+            scores = jnp.where(visible, scores, -jnp.inf)
+            highest = jnp.max(scores, axis=1, keepdims=True)
+            raised = jnp.exp(scores - highest)
+            weights = (raised / jnp.sum(raised, axis=1, keepdims=True)).astype(jnp.bfloat16)
+            out_wide[pl.ds(g, group_len, stride=tile), :] = jnp.dot(
+                weights, values[pair], preferred_element_type=jnp.float32
+            )
+        out_send[c] = out_wide[...].reshape(group_len, tile, hdim).astype(jnp.bfloat16)
+        for step in range(1, peers):
+            out_copy(c, step).start()
+        out_own(c).start()
+        if c:
+            forward_arrival(c - 1, 0).wait_recv()
+            forward(c - 1, 2).start()
+
+    forward_arrival(chunks - 1, 0).wait_recv()
+    forward(chunks - 1, 2).start()
+    for c in range(chunks):
+        for step in range(1, peers):
+            in_copy(c, step).wait_send()
+            out_copy(c, step).wait_send()
+            out_arrival(c, step).wait_recv()
+        out_own(c).wait()
+        keep(c).wait()
+        forward(c, 0).wait_send()
+        for kind in (1, 2):
+            forward(c, kind).wait_send()
+            forward_arrival(c, kind).wait_recv()
+
+
+def fused(fresh_qkv, stale_kv, valid_counts, text_len):
+    peers = lax.axis_size("seq")
+    _, rows, pair_count, hdim = fresh_qkv.shape
+    pairs_here = pair_count // peers
+    chunks = pairs_here // PAIR_TILE
+    group_len = rows * peers
+    seq_len = stale_kv.shape[1]
+    bf16, f32 = jnp.bfloat16, jnp.float32
+    fresh_blocks = fresh_qkv.reshape(3, rows, peers, chunks, PAIR_TILE, hdim)
+    stale_blocks = stale_kv.reshape(2, seq_len, chunks, PAIR_TILE, hdim)
+    dma = pltpu.SemaphoreType.DMA
+    attended, refreshed = pl.pallas_call(
+        functools.partial(fused_kernel, text_len),
+        out_shape=(
+            jax.ShapeDtypeStruct((rows, peers, chunks, PAIR_TILE, hdim), bf16),
+            jax.ShapeDtypeStruct(stale_blocks.shape, bf16),
+        ),
+        in_specs=[
+            pl.BlockSpec(memory_space=pltpu.SMEM),
+            pl.BlockSpec(memory_space=pl.ANY),
+            pl.BlockSpec(memory_space=pl.ANY),
+        ],
+        out_specs=(pl.BlockSpec(memory_space=pl.ANY), pl.BlockSpec(memory_space=pl.ANY)),
+        scratch_shapes=[
+            pltpu.VMEM((chunks, 3, group_len, PAIR_TILE, hdim), bf16),
+            pltpu.VMEM((2, chunks, seq_len, PAIR_TILE, hdim), bf16),
+            pltpu.VMEM((seq_len * PAIR_TILE, hdim), f32),
+            pltpu.VMEM((pairs_here, seq_len, hdim), bf16),
+            pltpu.VMEM((pairs_here, seq_len, hdim), bf16),
+            pltpu.VMEM((PAIR_TILE, group_len, hdim), bf16),
+            pltpu.VMEM((group_len * PAIR_TILE, hdim), f32),
+            pltpu.VMEM((chunks, group_len, PAIR_TILE, hdim), bf16),
+            dma((chunks, peers)),
+            dma((chunks, peers)),
+            dma((chunks,)),
+            dma((2, chunks)),
+            dma((3, chunks)),
+            dma((3, chunks)),
+            dma((chunks,)),
+            dma((chunks, peers)),
+            dma((chunks, peers)),
+            dma((chunks,)),
+        ],
+        compiler_params=pltpu.CompilerParams(
+            collective_id=0, has_side_effects=True, vmem_limit_bytes=48 * 1024 * 1024
+        ),
+        name="joint_attention",
+    )(valid_counts, fresh_blocks, stale_blocks)
+    return attended.reshape(rows, pair_count, hdim), refreshed.reshape(stale_kv.shape)
 
 
 def attend(query_part, key_part, value_part, valid_counts, text_len):
@@ -48,16 +319,18 @@
     patch_len = shard_rows * seq_count
     patch_index = lax.axis_index("patch")
     first_pair = lax.axis_index("seq") * pairs_here
+    seq_len = stale_kv.shape[1]
+    text_len = TXT_DEV * seq_len // (TXT_DEV + IMG_DEV)
+    image_index = (first_pair + jnp.arange(pairs_here)) // HEADS
+    matches = image_index[:, None] == jnp.arange(text_count.shape[0])[None, :]
+    valid_counts = jnp.sum(jnp.where(matches, text_count[None, :], 0), axis=1)
+    if pairs_here % PAIR_TILE == 0 and patch_len % 16 == 0 and lax.axis_size("patch") == 4:
+        return fused(fresh_qkv, stale_kv, valid_counts, text_len)
     exchanged = lax.all_to_all(fresh_qkv, "seq", split_axis=2, concat_axis=1, tiled=True)
     query_part = exchanged[0]
     own_kv = exchanged[1:]
     refreshed = lax.all_gather(own_kv, "patch", axis=1, tiled=True)
     merged_kv = lax.dynamic_update_slice_in_dim(stale_kv, own_kv, patch_index * patch_len, 1)
-    seq_len = stale_kv.shape[1]
-    text_len = TXT_DEV * seq_len // (TXT_DEV + IMG_DEV)
-    image_index = (first_pair + jnp.arange(pairs_here)) // HEADS
-    matches = image_index[:, None] == jnp.arange(text_count.shape[0])[None, :]
-    valid_counts = jnp.sum(jnp.where(matches, text_count[None, :], 0), axis=1)
     attended_part = attend(query_part, merged_kv[0], merged_kv[1], valid_counts, text_len)
     result = lax.all_to_all(attended_part, "seq", split_axis=0, concat_axis=1, tiled=True)
     return (result, refreshed)

time: 262 us -> 100 us (0.38)
  the two profiles are of different devices: /device:TPU:0 before, /device:TPU:13 now
where the time goes in v1:
time: 100 us
  Pallas kernels  88.8 us (89%)
  local copies, waits for them, and re-layouts  9.84 us (10%)
    pallas_call x1, Pallas kernels, fused(): pl.pallas_call(functools.partial(fused_kernel, text_len), out_shape=(jax....  88.8 us
    unnamed x4, local copies, waits for them, and re-layouts  9.84 us

profile of v1, /device:TPU:13, one launch (start us, length us, event | category | flops | bytes accessed | tf_op | source)
XLA Modules:
  0.0 100.1 jit_solution(3785517134886972617)
XLA Ops:
  0.7 0.7 select_reduce_fusion.counts_ref
  1.4 0.0 copy-start
  1.4 1.7 %copy-done = bf16[3,18,192,128]{3,2,1,0:T(8,128)(2,1)S(1)} copy-done((bf16[3,18,192,128]{3,2,1,0:T(8,128)(2,1)S(1)}, bf16[3,18,192,128]{3,2,1,0:T(8,128)(2,1)}, u32[]{:S(2)}) %copy-start) | copy-done | bytes 2654232
  3.1 88.8 %joint_attention.1 = (bf16[18,8,3,8,128]{4,3,2,1,0:T(8,128)(2,1)S(1)}, bf16[2,576,3,8,128]{4,3,2,1,0:T(8,128)(2,1)}) custom-call(s32[24]{0:T(128)S(1)} %select_reduce_fusion.counts_ref, bf16[3,18,8,3,8,128]{5,4,3,2,1,0:T(8,128)(2,1)S(1)} %bitcast.4, bf16[2,576,3,8,128]{4,3,2,1,0:T(8,128)(2,1)} %bitcast.6), custom_call_target="tpu_custom_call" | custom-call | tf_op jit(solution)/shard_map/joint_attention/pallas_call | solution.py:244
  92.0 0.9 copy.7
  92.9 7.2 %copy.8 = bf16[2,576,24,128]{3,2,1,0:T(8,128)(2,1)} copy(bf16[2,576,24,128]{3,2,1,0:T(8,128)(2,1)} %bitcast.7) | data formatting | bytes 14155776
  (1 shorter events, 0.0 us)
Async XLA Ops:
  1.4 1.7 %copy-start = (bf16[3,18,192,128]{3,2,1,0:T(8,128)(2,1)S(1)}, bf16[3,18,192,128]{3,2,1,0:T(8,128)(2,1)}, u32[]{:S(2)}) copy-start(bf16[3,18,192,128]{3,2,1,0:T(8,128)(2,1)} %param.3) | copy-start | bytes 7962628

commit v2 on v1

--- a/solution.py
+++ b/solution.py
@@ -22,6 +22,7 @@
     stale_ref,
     attended_ref,
     refreshed_ref,
+    counts,
     recv,
     stale_vmem,
     wide,
@@ -30,6 +31,7 @@
     queries,
     out_wide,
     out_send,
+    counts_sem,
     in_send_sem,
     in_recv_sem,
     own_sem,
@@ -58,6 +60,8 @@
     for twin in (core_twin, x_twin):
         pl.semaphore_signal(barrier, inc=1, device_id=(twin, s), device_id_type=MESH)
 
+    counts_copy = pltpu.make_async_copy(counts_ref, counts, counts_sem.at[0])
+    counts_copy.start()
     stale_copies = []
     for c in range(chunks):
         for which in range(2):
@@ -158,10 +162,16 @@
             out_send.at[c, pl.ds(rows * s, rows)], attended_ref.at[:, s, c], out_own_sem.at[c]
         )
 
-    for c in range(chunks):
+    def follow(c):
         for step in range(1, peers):
-            in_copy(c, step).start()
-
+            in_copy(c, step).wait_send()
+            if c + 1 < chunks:
+                in_copy(c + 1, step).start()
+
+    for step in range(1, peers):
+        in_copy(0, step).start()
+
+    counts_copy.wait()
     for copy in stale_copies:
         copy.wait()
     for c in range(chunks):
@@ -172,6 +182,7 @@
 
     position = lax.broadcasted_iota(jnp.int32, (1, seq_len), 1)
     for c in range(chunks):
+        follow(c)
         own_copies[c].wait()
         for step in range(1, peers):
             in_arrival(c, step).wait_recv()
@@ -199,7 +210,8 @@
                 )
                 * scale
             )
-            visible = (position >= text_len) | (position < counts_ref[pair])
+            image = (s * (chunks * tile) + pair) // HEADS
+            visible = (position >= text_len) | (position < counts[image])
             scores = jnp.where(visible, scores, -jnp.inf)
             highest = jnp.max(scores, axis=1, keepdims=True)
             raised = jnp.exp(scores - highest)
@@ -219,7 +231,6 @@
     forward(chunks - 1, 2).start()
     for c in range(chunks):
         for step in range(1, peers):
-            in_copy(c, step).wait_send()
             out_copy(c, step).wait_send()
             out_arrival(c, step).wait_recv()
         out_own(c).wait()
@@ -230,7 +241,25 @@
             forward_arrival(c, kind).wait_recv()
 
 
-def fused(fresh_qkv, stale_kv, valid_counts, text_len):
+def finish_kernel(attended_ref, refreshed_ref, attended_out, refreshed_out, sems):
+    copies = [pltpu.make_async_copy(attended_ref, attended_out, sems.at[0, 0])]
+    parts = 4
+    length = refreshed_ref.shape[1] // parts
+    for which in range(2):
+        for part in range(parts):
+            place = (which, pl.ds(part * length, length))
+            copies.append(
+                pltpu.make_async_copy(
+                    refreshed_ref.at[place], refreshed_out.at[place], sems.at[1 + which, part]
+                )
+            )
+    for copy in copies:
+        copy.start()
+    for copy in copies:
+        copy.wait()
+
+
+def fused(fresh_qkv, stale_kv, text_count, text_len):
     peers = lax.axis_size("seq")
     _, rows, pair_count, hdim = fresh_qkv.shape
     pairs_here = pair_count // peers
@@ -240,20 +269,20 @@
     bf16, f32 = jnp.bfloat16, jnp.float32
     fresh_blocks = fresh_qkv.reshape(3, rows, peers, chunks, PAIR_TILE, hdim)
     stale_blocks = stale_kv.reshape(2, seq_len, chunks, PAIR_TILE, hdim)
+    attended_shape = (rows, peers, chunks, PAIR_TILE, hdim)
     dma = pltpu.SemaphoreType.DMA
+    in_hbm = pl.BlockSpec(memory_space=pltpu.HBM)
+    anywhere = pl.BlockSpec(memory_space=pl.ANY)
     attended, refreshed = pl.pallas_call(
         functools.partial(fused_kernel, text_len),
         out_shape=(
-            jax.ShapeDtypeStruct((rows, peers, chunks, PAIR_TILE, hdim), bf16),
-            jax.ShapeDtypeStruct(stale_blocks.shape, bf16),
+            pltpu.VMEM(attended_shape, bf16),
+            pltpu.VMEM(stale_blocks.shape, bf16),
         ),
-        in_specs=[
-            pl.BlockSpec(memory_space=pltpu.SMEM),
-            pl.BlockSpec(memory_space=pl.ANY),
-            pl.BlockSpec(memory_space=pl.ANY),
-        ],
-        out_specs=(pl.BlockSpec(memory_space=pl.ANY), pl.BlockSpec(memory_space=pl.ANY)),
+        in_specs=[in_hbm, in_hbm, in_hbm],
+        out_specs=(anywhere, anywhere),
         scratch_shapes=[
+            pltpu.SMEM(text_count.shape, jnp.int32),
             pltpu.VMEM((chunks, 3, group_len, PAIR_TILE, hdim), bf16),
             pltpu.VMEM((2, chunks, seq_len, PAIR_TILE, hdim), bf16),
             pltpu.VMEM((seq_len * PAIR_TILE, hdim), f32),
@@ -262,6 +291,7 @@
             pltpu.VMEM((PAIR_TILE, group_len, hdim), bf16),
             pltpu.VMEM((group_len * PAIR_TILE, hdim), f32),
             pltpu.VMEM((chunks, group_len, PAIR_TILE, hdim), bf16),
+            dma((1,)),
             dma((chunks, peers)),
             dma((chunks, peers)),
             dma((chunks,)),
@@ -274,10 +304,25 @@
             dma((chunks,)),
         ],
         compiler_params=pltpu.CompilerParams(
-            collective_id=0, has_side_effects=True, vmem_limit_bytes=48 * 1024 * 1024
+            collective_id=0, has_side_effects=True, vmem_limit_bytes=32 * 1024 * 1024
         ),
         name="joint_attention",
-    )(valid_counts, fresh_blocks, stale_blocks)
+    )(
+        pltpu.with_memory_space_constraint(text_count, pltpu.HBM),
+        pltpu.with_memory_space_constraint(fresh_blocks, pltpu.HBM),
+        pltpu.with_memory_space_constraint(stale_blocks, pltpu.HBM),
+    )
+    attended, refreshed = pl.pallas_call(
+        finish_kernel,
+        out_shape=(
+            jax.ShapeDtypeStruct(attended_shape, bf16),
+            jax.ShapeDtypeStruct(stale_blocks.shape, bf16),
+        ),
+        in_specs=[anywhere, anywhere],
+        out_specs=(in_hbm, in_hbm),
+        scratch_shapes=[dma((3, 4))],
+        name="results_to_hbm",
+    )(attended, refreshed)
     return attended.reshape(rows, pair_count, hdim), refreshed.reshape(stale_kv.shape)
 
 
@@ -325,7 +370,7 @@
     matches = image_index[:, None] == jnp.arange(text_count.shape[0])[None, :]
     valid_counts = jnp.sum(jnp.where(matches, text_count[None, :], 0), axis=1)
     if pairs_here % PAIR_TILE == 0 and patch_len % 16 == 0 and lax.axis_size("patch") == 4:
-        return fused(fresh_qkv, stale_kv, valid_counts, text_len)
+        return fused(fresh_qkv, stale_kv, text_count, text_len)
     exchanged = lax.all_to_all(fresh_qkv, "seq", split_axis=2, concat_axis=1, tiled=True)
     query_part = exchanged[0]
     own_kv = exchanged[1:]

time: 100 us -> 337 us (3.37)
  the two profiles are of different devices: /device:TPU:13 before, /device:TPU:0 now
where the time goes in v2:
time: 337 us; the launch traced here: 333 us
  Pallas kernels  329 us (98%)
  local copies, waits for them, and re-layouts  3.82 us (1%)
    pallas_call x1, Pallas kernels, fused(): pl.pallas_call(finish_kernel, out_shape=(jax.ShapeDtypeStruct(attended_sh...  242 us
    pallas_call x1, Pallas kernels, fused(): pl.pallas_call(functools.partial(fused_kernel, text_len), out_shape=(pltp...  86.5 us

profile of v2, /device:TPU:0, one launch (start us, length us, event | category | flops | bytes accessed | tf_op | source)
XLA Modules:
  0.0 333.4 jit_solution(7202363982166356749)
XLA Ops:
  0.6 86.5 %joint_attention.1 = (bf16[18,8,3,8,128]{4,3,2,1,0:T(8,128)(2,1)S(1)}, bf16[2,576,3,8,128]{4,3,2,1,0:T(8,128)(2,1)S(1)}) custom-call(s32[8]{0:T(128)} %counts_ref.1, bf16[3,18,8,3,8,128]{5,4,3,2,1,0:T(8,128)(2,1)} %bitcast.5, bf16[2,576,3,8,128]{4,3,2,1,0:T(8,128)(2,1)} %bitcast.4), custom_call_target="tpu_custom_call" | custom-call | tf_op jit(solution)/shard_map/joint_attention/pallas_call | solution.py:276
  87.2 0.0 copy-start
  87.2 2.9 copy-done
  90.1 0.0 copy-start.1
  90.1 0.9 copy-done.1
  91.0 242.4 %results_to_hbm.1 = (bf16[18,8,3,8,128]{4,3,2,1,0:T(8,128)(2,1)}, bf16[2,576,3,8,128]{4,3,2,1,0:T(8,128)(2,1)}) custom-call(bf16[18,8,3,8,128]{4,3,2,1,0:T(8,128)(2,1)} %copy-done.1, bf16[2,576,3,8,128]{4,3,2,1,0:T(8,128)(2,1)} %copy-done), custom_call_target="tpu_custom_call" | custom-call | tf_op jit(solution)/shard_map/results_to_hbm/pallas_call | solution.py:315
Async XLA Ops:
  87.2 2.9 copy-start
  90.1 0.9 copy-start.1

commit v3 on v2

--- a/solution.py
+++ b/solution.py
@@ -79,24 +79,30 @@
         own_copies.append(copy)
     pl.semaphore_wait(barrier, peers + 1)
 
-    def in_copy(c, step):
+    groups = [(0, 1, 2), (0, 0, 1)]
+    groups += [(c, 1, 2) for c in range(1, chunks)]
+    groups += [(c, 0, 1) for c in range(1, chunks)]
+
+    def in_copy(k, step):
+        c, first, count = groups[k]
         to = (s + step) % peers
         return pltpu.make_async_remote_copy(
-            src_ref=fresh_ref.at[:, :, to, c],
-            dst_ref=recv.at[c, :, pl.ds(rows * s, rows)],
-            send_sem=in_send_sem.at[c, step],
-            recv_sem=in_recv_sem.at[c, step],
+            src_ref=fresh_ref.at[pl.ds(first, count), :, to, c],
+            dst_ref=recv.at[c, pl.ds(first, count), pl.ds(rows * s, rows)],
+            send_sem=in_send_sem.at[k, step],
+            recv_sem=in_recv_sem.at[k, step],
             device_id=(p, to),
             device_id_type=MESH,
         )
 
-    def in_arrival(c, step):
+    def in_arrival(k, step):
+        c, first, count = groups[k]
         origin = (s + peers - step) % peers
         return pltpu.make_async_remote_copy(
-            src_ref=fresh_ref.at[:, :, origin, c],
-            dst_ref=recv.at[c, :, pl.ds(rows * origin, rows)],
-            send_sem=in_send_sem.at[c, step],
-            recv_sem=in_recv_sem.at[c, step],
+            src_ref=fresh_ref.at[pl.ds(first, count), :, origin, c],
+            dst_ref=recv.at[c, pl.ds(first, count), pl.ds(rows * origin, rows)],
+            send_sem=in_send_sem.at[k, step],
+            recv_sem=in_recv_sem.at[k, step],
             device_id=(p, origin),
             device_id_type=MESH,
         )
@@ -162,14 +168,15 @@
             out_send.at[c, pl.ds(rows * s, rows)], attended_ref.at[:, s, c], out_own_sem.at[c]
         )
 
-    def follow(c):
-        for step in range(1, peers):
-            in_copy(c, step).wait_send()
-            if c + 1 < chunks:
-                in_copy(c + 1, step).start()
-
-    for step in range(1, peers):
-        in_copy(0, step).start()
+    def follow(k):
+        for step in range(1, peers):
+            in_copy(k, step).wait_send()
+            if k + 2 < len(groups):
+                in_copy(k + 2, step).start()
+
+    for k in range(2):
+        for step in range(1, peers):
+            in_copy(k, step).start()
 
     counts_copy.wait()
     for copy in stale_copies:
@@ -180,42 +187,44 @@
             for g in range(tile):
                 target[c * tile + g] = wide[pl.ds(g, seq_len, stride=tile), :].astype(jnp.bfloat16)
 
-    position = lax.broadcasted_iota(jnp.int32, (1, seq_len), 1)
-    for c in range(chunks):
-        follow(c)
-        own_copies[c].wait()
-        for step in range(1, peers):
-            in_arrival(c, step).wait_recv()
+    masked_lanes = min(seq_len, -(-text_len // 128) * 128)
+    position = lax.broadcasted_iota(jnp.int32, (1, masked_lanes), 1)
+
+    def rows_of_pairs(c, which):
+        part = wide.at[pl.ds(0, group_len * tile)]
+        part[...] = recv[c, which].astype(jnp.float32).reshape(group_len * tile, hdim)
+        return [
+            part[pl.ds(g, group_len, stride=tile), :].astype(jnp.bfloat16) for g in range(tile)
+        ]
+
+    def take_keys(c):
         forward(c, 0).start()
         forward(c, 1).start()
         keep(c).start()
-        for which, target in ((0, queries), (1, keys), (2, values)):
-            part = wide.at[pl.ds(0, group_len * tile)]
-            part[...] = recv[c, which].astype(jnp.float32).reshape(group_len * tile, hdim)
-            for g in range(tile):
-                block = part[pl.ds(g, group_len, stride=tile), :].astype(jnp.bfloat16)
-                if which == 0:
-                    target[g] = block
-                else:
-                    target[c * tile + g, pl.ds(pl.multiple_of(group_len * p, 16), group_len), :] = block
-
+        place = pl.ds(pl.multiple_of(group_len * p, 16), group_len)
+        for which, target in ((1, keys), (2, values)):
+            for g, block in enumerate(rows_of_pairs(c, which)):
+                target[c * tile + g, place, :] = block
+
+    def attend_chunk(c):
+        for g, query in enumerate(rows_of_pairs(c, 0)):
+            queries[g] = query
         for g in range(tile):
             pair = c * tile + g
-            scores = (
-                lax.dot_general(
-                    queries[g],
-                    keys[pair],
-                    (((1,), (1,)), ((), ())),
-                    preferred_element_type=jnp.float32,
-                )
-                * scale
+            scores = lax.dot_general(
+                queries[g], keys[pair], (((1,), (1,)), ((), ())), preferred_element_type=jnp.float32
             )
             image = (s * (chunks * tile) + pair) // HEADS
             visible = (position >= text_len) | (position < counts[image])
-            scores = jnp.where(visible, scores, -jnp.inf)
+            text_scores = jnp.where(visible, scores[:, :masked_lanes], -jnp.inf)
+            if masked_lanes < seq_len:
+                scores = jnp.concatenate([text_scores, scores[:, masked_lanes:]], axis=1)
+            else:
+                scores = text_scores
             highest = jnp.max(scores, axis=1, keepdims=True)
-            raised = jnp.exp(scores - highest)
-            weights = (raised / jnp.sum(raised, axis=1, keepdims=True)).astype(jnp.bfloat16)
+            raised = jnp.exp2((scores - highest) * (scale * math.log2(math.e)))
+            total = jnp.sum(raised, axis=1, keepdims=True)
+            weights = (raised * (1.0 / total)).astype(jnp.bfloat16)
             out_wide[pl.ds(g, group_len, stride=tile), :] = jnp.dot(
                 weights, values[pair], preferred_element_type=jnp.float32
             )
@@ -223,9 +232,22 @@
         for step in range(1, peers):
             out_copy(c, step).start()
         out_own(c).start()
-        if c:
-            forward_arrival(c - 1, 0).wait_recv()
-            forward(c - 1, 2).start()
+
+    relays = 0
+    for copy in own_copies:
+        copy.wait()
+    for k, (c, first, _) in enumerate(groups):
+        follow(k)
+        for step in range(1, peers):
+            in_arrival(k, step).wait_recv()
+        if first == 1:
+            take_keys(c)
+        else:
+            attend_chunk(c)
+        if k >= 2 and relays + 1 < chunks:
+            forward_arrival(relays, 0).wait_recv()
+            forward(relays, 2).start()
+            relays += 1
 
     forward_arrival(chunks - 1, 0).wait_recv()
     forward(chunks - 1, 2).start()
@@ -239,24 +261,6 @@
         for kind in (1, 2):
             forward(c, kind).wait_send()
             forward_arrival(c, kind).wait_recv()
-
-
-def finish_kernel(attended_ref, refreshed_ref, attended_out, refreshed_out, sems):
-    copies = [pltpu.make_async_copy(attended_ref, attended_out, sems.at[0, 0])]
-    parts = 4
-    length = refreshed_ref.shape[1] // parts
-    for which in range(2):
-        for part in range(parts):
-            place = (which, pl.ds(part * length, length))
-            copies.append(
-                pltpu.make_async_copy(
-                    refreshed_ref.at[place], refreshed_out.at[place], sems.at[1 + which, part]
-                )
-            )
-    for copy in copies:
-        copy.start()
-    for copy in copies:
-        copy.wait()
 
 
 def fused(fresh_qkv, stale_kv, text_count, text_len):
@@ -292,8 +296,8 @@
             pltpu.VMEM((group_len * PAIR_TILE, hdim), f32),
             pltpu.VMEM((chunks, group_len, PAIR_TILE, hdim), bf16),
             dma((1,)),
-            dma((chunks, peers)),
-            dma((chunks, peers)),
+            dma((2 * chunks, peers)),
+            dma((2 * chunks, peers)),
             dma((chunks,)),
             dma((2, chunks)),
             dma((3, chunks)),
@@ -312,17 +316,6 @@
         pltpu.with_memory_space_constraint(fresh_blocks, pltpu.HBM),
         pltpu.with_memory_space_constraint(stale_blocks, pltpu.HBM),
     )
-    attended, refreshed = pl.pallas_call(
-        finish_kernel,
-        out_shape=(
-            jax.ShapeDtypeStruct(attended_shape, bf16),
-            jax.ShapeDtypeStruct(stale_blocks.shape, bf16),
-        ),
-        in_specs=[anywhere, anywhere],
-        out_specs=(in_hbm, in_hbm),
-        scratch_shapes=[dma((3, 4))],
-        name="results_to_hbm",
-    )(attended, refreshed)
     return attended.reshape(rows, pair_count, hdim), refreshed.reshape(stale_kv.shape)
 
 

time: 337 us -> 89.6 us (0.27); the launches traced: 333 us -> 89.5 us
  Pallas kernels: 329 us -> 85 us
    pallas_call x1 -> x0, Pallas kernels: 242 us -> none  [fused(): pl.pallas_call(finish_kernel, out_shape=(jax.ShapeDtypeStruct(attended_sh...]
where the time goes in v3:
time: 89.6 us; the launch traced here: 89.5 us
  Pallas kernels  85 us (95%)
  local copies, waits for them, and re-layouts  3.88 us (4%)
    pallas_call x1, Pallas kernels, fused(): pl.pallas_call(functools.partial(fused_kernel, text_len), out_shape=(pltp...  85 us
    unnamed x2, local copies, waits for them, and re-layouts  3.88 us

profile of v3, /device:TPU:0, one launch (start us, length us, event | category | flops | bytes accessed | tf_op | source)
XLA Modules:
  0.0 89.5 jit_solution(10435803414236763214)
XLA Ops:
  0.6 85.0 %joint_attention.1 = (bf16[18,8,3,8,128]{4,3,2,1,0:T(8,128)(2,1)S(1)}, bf16[2,576,3,8,128]{4,3,2,1,0:T(8,128)(2,1)S(1)}) custom-call(s32[8]{0:T(128)} %counts_ref.1, bf16[3,18,8,3,8,128]{5,4,3,2,1,0:T(8,128)(2,1)} %bitcast.7, bf16[2,576,3,8,128]{4,3,2,1,0:T(8,128)(2,1)} %bitcast.6), custom_call_target="tpu_custom_call" | custom-call | tf_op jit(solution)/shard_map/joint_attention/pallas_call | solution.py:280
  85.6 0.9 %copy.7 = bf16[18,192,128]{2,1,0:T(8,128)(2,1)} copy(bf16[18,192,128]{2,1,0:T(8,128)(2,1)S(1)} %bitcast.5) | data formatting | bytes 1769472
  86.5 3.0 %copy.8 = bf16[2,576,24,128]{3,2,1,0:T(8,128)(2,1)} copy(bf16[2,576,24,128]{3,2,1,0:T(8,128)(2,1)S(1)} %bitcast.4) | data formatting | bytes 14155776

commit v4 on v3

--- a/solution.py
+++ b/solution.py
@@ -60,6 +60,117 @@
     for twin in (core_twin, x_twin):
         pl.semaphore_signal(barrier, inc=1, device_id=(twin, s), device_id_type=MESH)
 
+    pl.semaphore_wait(barrier, peers + 1)
+
+    groups = [(0, 1, 2), (0, 0, 1)]
+    groups += [(c, 1, 2) for c in range(1, chunks)]
+    groups += [(c, 0, 1) for c in range(1, chunks)]
+
+    def in_copy(k, step):
+        c, first, count = groups[k]
+        to = (s + step) % peers
+        return pltpu.make_async_remote_copy(
+            src_ref=fresh_ref.at[pl.ds(first, count), :, to, c],
+            dst_ref=recv.at[c, pl.ds(first, count), pl.ds(rows * s, rows)],
+            send_sem=in_send_sem.at[k, step],
+            recv_sem=in_recv_sem.at[k, step],
+            device_id=(p, to),
+            device_id_type=MESH,
+        )
+
+    def in_arrival(k, step):
+        c, first, count = groups[k]
+        origin = (s + peers - step) % peers
+        return pltpu.make_async_remote_copy(
+            src_ref=fresh_ref.at[pl.ds(first, count), :, origin, c],
+            dst_ref=recv.at[c, pl.ds(first, count), pl.ds(rows * origin, rows)],
+            send_sem=in_send_sem.at[k, step],
+            recv_sem=in_recv_sem.at[k, step],
+            device_id=(p, origin),
+            device_id_type=MESH,
+        )
+
+    def forward(c, kind):
+        if kind == 2:
+            place = refreshed_ref.at[:, pl.ds(group_len * x_twin, group_len), c]
+            source = place
+        else:
+            place = refreshed_ref.at[:, pl.ds(group_len * p, group_len), c]
+            source = recv.at[c, pl.ds(1, 2)]
+        return pltpu.make_async_remote_copy(
+            src_ref=source,
+            dst_ref=place,
+            send_sem=fwd_send_sem.at[kind, c],
+            recv_sem=fwd_recv_sem.at[kind, c],
+            device_id=(x_twin if kind == 0 else core_twin, s),
+            device_id_type=MESH,
+        )
+
+    def forward_arrival(c, kind):
+        origin = {0: x_twin, 1: core_twin, 2: (core_twin + 2) % 4}[kind]
+        return pltpu.make_async_remote_copy(
+            src_ref=recv.at[c, pl.ds(1, 2)],
+            dst_ref=refreshed_ref.at[:, pl.ds(group_len * origin, group_len), c],
+            send_sem=fwd_send_sem.at[kind, c],
+            recv_sem=fwd_recv_sem.at[kind, c],
+            device_id=(x_twin if kind == 0 else core_twin, s),
+            device_id_type=MESH,
+        )
+
+    def keep(c):
+        return pltpu.make_async_copy(
+            recv.at[c, pl.ds(1, 2)],
+            refreshed_ref.at[:, pl.ds(group_len * p, group_len), c],
+            keep_sem.at[c],
+        )
+
+    half = peers // 2
+    near = s // half
+
+    def out_peer(c, slot, sign):
+        if c + 1 < chunks:
+            return (s + peers + sign * slot) % peers
+        if slot < half:
+            return near * half + (s % half + half + sign * slot) % half
+        return (1 - near) * half + (s % half + half + sign * (slot - half)) % half
+
+    def out_copy(c, slot):
+        to = out_peer(c, slot, 1)
+        return pltpu.make_async_remote_copy(
+            src_ref=out_send.at[c, pl.ds(rows * to, rows)],
+            dst_ref=attended_ref.at[:, s, c],
+            send_sem=out_send_sem.at[c, slot],
+            recv_sem=out_recv_sem.at[c, slot],
+            device_id=(p, to),
+            device_id_type=MESH,
+        )
+
+    def out_arrival(c, slot):
+        origin = out_peer(c, slot, -1)
+        return pltpu.make_async_remote_copy(
+            src_ref=out_send.at[c, pl.ds(rows * origin, rows)],
+            dst_ref=attended_ref.at[:, origin, c],
+            send_sem=out_send_sem.at[c, slot],
+            recv_sem=out_recv_sem.at[c, slot],
+            device_id=(p, origin),
+            device_id_type=MESH,
+        )
+
+    def out_own(c):
+        return pltpu.make_async_copy(
+            out_send.at[c, pl.ds(rows * s, rows)], attended_ref.at[:, s, c], out_own_sem.at[c]
+        )
+
+    flight = 3
+
+    def follow(k):
+        for step in range(1, peers):
+            in_copy(k, step).wait_send()
+            if k + flight < len(groups):
+                in_copy(k + flight, step).start()
+
+    for step in range(1, peers):
+        in_copy(0, step).start()
     counts_copy = pltpu.make_async_copy(counts_ref, counts, counts_sem.at[0])
     counts_copy.start()
     stale_copies = []
@@ -77,104 +188,7 @@
         )
         copy.start()
         own_copies.append(copy)
-    pl.semaphore_wait(barrier, peers + 1)
-
-    groups = [(0, 1, 2), (0, 0, 1)]
-    groups += [(c, 1, 2) for c in range(1, chunks)]
-    groups += [(c, 0, 1) for c in range(1, chunks)]
-
-    def in_copy(k, step):
-        c, first, count = groups[k]
-        to = (s + step) % peers
-        return pltpu.make_async_remote_copy(
-            src_ref=fresh_ref.at[pl.ds(first, count), :, to, c],
-            dst_ref=recv.at[c, pl.ds(first, count), pl.ds(rows * s, rows)],
-            send_sem=in_send_sem.at[k, step],
-            recv_sem=in_recv_sem.at[k, step],
-            device_id=(p, to),
-            device_id_type=MESH,
-        )
-
-    def in_arrival(k, step):
-        c, first, count = groups[k]
-        origin = (s + peers - step) % peers
-        return pltpu.make_async_remote_copy(
-            src_ref=fresh_ref.at[pl.ds(first, count), :, origin, c],
-            dst_ref=recv.at[c, pl.ds(first, count), pl.ds(rows * origin, rows)],
-            send_sem=in_send_sem.at[k, step],
-            recv_sem=in_recv_sem.at[k, step],
-            device_id=(p, origin),
-            device_id_type=MESH,
-        )
-
-    def forward(c, kind):
-        if kind == 2:
-            place = refreshed_ref.at[:, pl.ds(group_len * x_twin, group_len), c]
-            source = place
-        else:
-            place = refreshed_ref.at[:, pl.ds(group_len * p, group_len), c]
-            source = recv.at[c, pl.ds(1, 2)]
-        return pltpu.make_async_remote_copy(
-            src_ref=source,
-            dst_ref=place,
-            send_sem=fwd_send_sem.at[kind, c],
-            recv_sem=fwd_recv_sem.at[kind, c],
-            device_id=(x_twin if kind == 0 else core_twin, s),
-            device_id_type=MESH,
-        )
-
-    def forward_arrival(c, kind):
-        origin = {0: x_twin, 1: core_twin, 2: (core_twin + 2) % 4}[kind]
-        return pltpu.make_async_remote_copy(
-            src_ref=recv.at[c, pl.ds(1, 2)],
-            dst_ref=refreshed_ref.at[:, pl.ds(group_len * origin, group_len), c],
-            send_sem=fwd_send_sem.at[kind, c],
-            recv_sem=fwd_recv_sem.at[kind, c],
-            device_id=(x_twin if kind == 0 else core_twin, s),
-            device_id_type=MESH,
-        )
-
-    def keep(c):
-        return pltpu.make_async_copy(
-            recv.at[c, pl.ds(1, 2)],
-            refreshed_ref.at[:, pl.ds(group_len * p, group_len), c],
-            keep_sem.at[c],
-        )
-
-    def out_copy(c, step):
-        to = (s + step) % peers
-        return pltpu.make_async_remote_copy(
-            src_ref=out_send.at[c, pl.ds(rows * to, rows)],
-            dst_ref=attended_ref.at[:, s, c],
-            send_sem=out_send_sem.at[c, step],
-            recv_sem=out_recv_sem.at[c, step],
-            device_id=(p, to),
-            device_id_type=MESH,
-        )
-
-    def out_arrival(c, step):
-        origin = (s + peers - step) % peers
-        return pltpu.make_async_remote_copy(
-            src_ref=out_send.at[c, pl.ds(rows * origin, rows)],
-            dst_ref=attended_ref.at[:, origin, c],
-            send_sem=out_send_sem.at[c, step],
-            recv_sem=out_recv_sem.at[c, step],
-            device_id=(p, origin),
-            device_id_type=MESH,
-        )
-
-    def out_own(c):
-        return pltpu.make_async_copy(
-            out_send.at[c, pl.ds(rows * s, rows)], attended_ref.at[:, s, c], out_own_sem.at[c]
-        )
-
-    def follow(k):
-        for step in range(1, peers):
-            in_copy(k, step).wait_send()
-            if k + 2 < len(groups):
-                in_copy(k + 2, step).start()
-
-    for k in range(2):
+    for k in range(1, min(flight, len(groups))):
         for step in range(1, peers):
             in_copy(k, step).start()
 
@@ -190,12 +204,11 @@
     masked_lanes = min(seq_len, -(-text_len // 128) * 128)
     position = lax.broadcasted_iota(jnp.int32, (1, masked_lanes), 1)
 
-    def rows_of_pairs(c, which):
-        part = wide.at[pl.ds(0, group_len * tile)]
-        part[...] = recv[c, which].astype(jnp.float32).reshape(group_len * tile, hdim)
-        return [
-            part[pl.ds(g, group_len, stride=tile), :].astype(jnp.bfloat16) for g in range(tile)
-        ]
+    def rows_of_pairs(c, which, start=0, count=group_len):
+        part = wide.at[pl.ds(0, count * tile)]
+        block = recv[c, which, pl.ds(start, count)]
+        part[...] = block.astype(jnp.float32).reshape(count * tile, hdim)
+        return [part[pl.ds(g, count, stride=tile), :].astype(jnp.bfloat16) for g in range(tile)]
 
     def take_keys(c):
         forward(c, 0).start()
@@ -206,13 +219,13 @@
             for g, block in enumerate(rows_of_pairs(c, which)):
                 target[c * tile + g, place, :] = block
 
-    def attend_chunk(c):
-        for g, query in enumerate(rows_of_pairs(c, 0)):
-            queries[g] = query
+    def attend_rows(c, start, count):
+        for g, query in enumerate(rows_of_pairs(c, 0, start, count)):
+            queries[g, :count] = query
         for g in range(tile):
             pair = c * tile + g
             scores = lax.dot_general(
-                queries[g], keys[pair], (((1,), (1,)), ((), ())), preferred_element_type=jnp.float32
+                queries[g, :count], keys[pair], (((1,), (1,)), ((), ())), preferred_element_type=jnp.float32
             )
             image = (s * (chunks * tile) + pair) // HEADS
             visible = (position >= text_len) | (position < counts[image])
@@ -225,12 +238,29 @@
             raised = jnp.exp2((scores - highest) * (scale * math.log2(math.e)))
             total = jnp.sum(raised, axis=1, keepdims=True)
             weights = (raised * (1.0 / total)).astype(jnp.bfloat16)
-            out_wide[pl.ds(g, group_len, stride=tile), :] = jnp.dot(
+            out_wide[pl.ds(g, count, stride=tile), :] = jnp.dot(
                 weights, values[pair], preferred_element_type=jnp.float32
             )
-        out_send[c] = out_wide[...].reshape(group_len, tile, hdim).astype(jnp.bfloat16)
-        for step in range(1, peers):
-            out_copy(c, step).start()
+        block = out_wide[: count * tile].reshape(count, tile, hdim).astype(jnp.bfloat16)
+        out_send[c, pl.ds(start, count)] = block
+
+    def relay(c):
+        forward_arrival(c, 0).wait_recv()
+        forward(c, 2).start()
+
+    def attend_chunk(c):
+        if c + 1 < chunks:
+            attend_rows(c, 0, group_len)
+            for slot in range(1, peers):
+                out_copy(c, slot).start()
+        else:
+            attend_rows(c, (1 - near) * (rows * half), rows * half)
+            for slot in range(half, peers):
+                out_copy(c, slot).start()
+            relay(c)
+            attend_rows(c, near * (rows * half), rows * half)
+            for slot in range(1, half):
+                out_copy(c, slot).start()
         out_own(c).start()
 
     relays = 0
@@ -245,12 +275,9 @@
         else:
             attend_chunk(c)
         if k >= 2 and relays + 1 < chunks:
-            forward_arrival(relays, 0).wait_recv()
-            forward(relays, 2).start()
+            relay(relays)
             relays += 1
 
-    forward_arrival(chunks - 1, 0).wait_recv()
-    forward(chunks - 1, 2).start()
     for c in range(chunks):
         for step in range(1, peers):
             out_copy(c, step).wait_send()
@@ -362,7 +389,8 @@
     image_index = (first_pair + jnp.arange(pairs_here)) // HEADS
     matches = image_index[:, None] == jnp.arange(text_count.shape[0])[None, :]
     valid_counts = jnp.sum(jnp.where(matches, text_count[None, :], 0), axis=1)
-    if pairs_here % PAIR_TILE == 0 and patch_len % 16 == 0 and lax.axis_size("patch") == 4:
+    halves = seq_count % 2 == 0 and patch_len % 16 == 0
+    if pairs_here % PAIR_TILE == 0 and halves and lax.axis_size("patch") == 4:
         return fused(fresh_qkv, stale_kv, text_count, text_len)
     exchanged = lax.all_to_all(fresh_qkv, "seq", split_axis=2, concat_axis=1, tiled=True)
     query_part = exchanged[0]

time: 89.6 us -> 95.2 us (1.062)
  Pallas kernels: 85 us -> 90.5 us
    pallas_call x1, Pallas kernels: 85 us -> 90.5 us  [fused(): pl.pallas_call(functools.partial(fused_kernel, text_len), out_shape=(pltp...]
where the time goes in v4:
time: 95.2 us; the launch traced here: 95 us
  Pallas kernels  90.5 us (95%)
  local copies, waits for them, and re-layouts  3.88 us (4%)
    pallas_call x1, Pallas kernels, fused(): pl.pallas_call(functools.partial(fused_kernel, text_len), out_shape=(pltp...  90.5 us
    unnamed x2, local copies, waits for them, and re-layouts  3.88 us

profile of v4, /device:TPU:0, one launch (start us, length us, event | category | flops | bytes accessed | tf_op | source)
XLA Modules:
  0.0 95.0 jit_solution(9339966517207293357)
XLA Ops:
  0.6 90.5 %joint_attention.1 = (bf16[18,8,3,8,128]{4,3,2,1,0:T(8,128)(2,1)S(1)}, bf16[2,576,3,8,128]{4,3,2,1,0:T(8,128)(2,1)S(1)}) custom-call(s32[8]{0:T(128)} %counts_ref.1, bf16[3,18,8,3,8,128]{5,4,3,2,1,0:T(8,128)(2,1)} %bitcast.7, bf16[2,576,3,8,128]{4,3,2,1,0:T(8,128)(2,1)} %bitcast.6), custom_call_target="tpu_custom_call" | custom-call | tf_op jit(solution)/shard_map/joint_attention/pallas_call | solution.py:307
  91.2 0.9 copy.7
  92.1 3.0 %copy.8 = bf16[2,576,24,128]{3,2,1,0:T(8,128)(2,1)} copy(bf16[2,576,24,128]{3,2,1,0:T(8,128)(2,1)S(1)} %bitcast.4) | data formatting | bytes 14155776

commit v5 on v3

--- a/solution.py
+++ b/solution.py
@@ -168,13 +168,16 @@
             out_send.at[c, pl.ds(rows * s, rows)], attended_ref.at[:, s, c], out_own_sem.at[c]
         )
 
+    last = len(groups) - 1
+
     def follow(k):
+        after = k + 1 if k == last - 1 else k + 2
         for step in range(1, peers):
             in_copy(k, step).wait_send()
-            if k + 2 < len(groups):
-                in_copy(k + 2, step).start()
-
-    for k in range(2):
+            if after < last or after == k + 1:
+                in_copy(after, step).start()
+
+    for k in range(min(2, last)):
         for step in range(1, peers):
             in_copy(k, step).start()
 
@@ -197,10 +200,12 @@
             part[pl.ds(g, group_len, stride=tile), :].astype(jnp.bfloat16) for g in range(tile)
         ]
 
-    def take_keys(c):
+    def send_keys(c):
         forward(c, 0).start()
         forward(c, 1).start()
         keep(c).start()
+
+    def store_keys(c):
         place = pl.ds(pl.multiple_of(group_len * p, 16), group_len)
         for which, target in ((1, keys), (2, values)):
             for g, block in enumerate(rows_of_pairs(c, which)):
@@ -234,14 +239,20 @@
         out_own(c).start()
 
     relays = 0
+    followed = []
     for copy in own_copies:
         copy.wait()
     for k, (c, first, _) in enumerate(groups):
-        follow(k)
+        if k not in followed:
+            follow(k)
         for step in range(1, peers):
             in_arrival(k, step).wait_recv()
         if first == 1:
-            take_keys(c)
+            send_keys(c)
+            if k == last - 2:
+                follow(k + 1)
+                followed.append(k + 1)
+            store_keys(c)
         else:
             attend_chunk(c)
         if k >= 2 and relays + 1 < chunks:

time: 89.6 us -> 89.6 us (level)
  no operation moved by 1% of the time
where the time goes in v5:
time: 89.6 us; the launch traced here: 89.5 us
  Pallas kernels  85 us (95%)
  local copies, waits for them, and re-layouts  3.88 us (4%)
    pallas_call x1, Pallas kernels, fused(): pl.pallas_call(functools.partial(fused_kernel, text_len), out_shape=(pltp...  85 us
    unnamed x2, local copies, waits for them, and re-layouts  3.88 us

profile of v5, /device:TPU:0, one launch (start us, length us, event | category | flops | bytes accessed | tf_op | source)
XLA Modules:
  0.0 89.5 jit_solution(18150101331774748006)
XLA Ops:
  0.6 85.0 %joint_attention.1 = (bf16[18,8,3,8,128]{4,3,2,1,0:T(8,128)(2,1)S(1)}, bf16[2,576,3,8,128]{4,3,2,1,0:T(8,128)(2,1)S(1)}) custom-call(s32[8]{0:T(128)} %counts_ref.1, bf16[3,18,8,3,8,128]{5,4,3,2,1,0:T(8,128)(2,1)} %bitcast.7, bf16[2,576,3,8,128]{4,3,2,1,0:T(8,128)(2,1)} %bitcast.6), custom_call_target="tpu_custom_call" | custom-call | tf_op jit(solution)/shard_map/joint_attention/pallas_call | solution.py:291
  85.6 0.9 %copy.7 = bf16[18,192,128]{2,1,0:T(8,128)(2,1)} copy(bf16[18,192,128]{2,1,0:T(8,128)(2,1)S(1)} %bitcast.5) | data formatting | bytes 1769472
  86.5 3.0 %copy.8 = bf16[2,576,24,128]{3,2,1,0:T(8,128)(2,1)} copy(bf16[2,576,24,128]{3,2,1,0:T(8,128)(2,1)S(1)} %bitcast.4) | data formatting | bytes 14155776

commit v6 on v3

--- a/solution.py
+++ b/solution.py
@@ -60,6 +60,105 @@
     for twin in (core_twin, x_twin):
         pl.semaphore_signal(barrier, inc=1, device_id=(twin, s), device_id_type=MESH)
 
+    pl.semaphore_wait(barrier, peers + 1)
+
+    groups = [(c, 1, 2) for c in range(chunks)] + [(c, 0, 1) for c in range(chunks)]
+
+    def in_copy(k, step):
+        c, first, count = groups[k]
+        to = (s + step) % peers
+        return pltpu.make_async_remote_copy(
+            src_ref=fresh_ref.at[pl.ds(first, count), :, to, c],
+            dst_ref=recv.at[c, pl.ds(first, count), pl.ds(rows * s, rows)],
+            send_sem=in_send_sem.at[k, step],
+            recv_sem=in_recv_sem.at[k, step],
+            device_id=(p, to),
+            device_id_type=MESH,
+        )
+
+    def in_arrival(k, step):
+        c, first, count = groups[k]
+        origin = (s + peers - step) % peers
+        return pltpu.make_async_remote_copy(
+            src_ref=fresh_ref.at[pl.ds(first, count), :, origin, c],
+            dst_ref=recv.at[c, pl.ds(first, count), pl.ds(rows * origin, rows)],
+            send_sem=in_send_sem.at[k, step],
+            recv_sem=in_recv_sem.at[k, step],
+            device_id=(p, origin),
+            device_id_type=MESH,
+        )
+
+    def forward(c, kind):
+        if kind == 2:
+            place = refreshed_ref.at[:, pl.ds(group_len * x_twin, group_len), c]
+            source = place
+        else:
+            place = refreshed_ref.at[:, pl.ds(group_len * p, group_len), c]
+            source = recv.at[c, pl.ds(1, 2)]
+        return pltpu.make_async_remote_copy(
+            src_ref=source,
+            dst_ref=place,
+            send_sem=fwd_send_sem.at[kind, c],
+            recv_sem=fwd_recv_sem.at[kind, c],
+            device_id=(x_twin if kind == 0 else core_twin, s),
+            device_id_type=MESH,
+        )
+
+    def forward_arrival(c, kind):
+        origin = {0: x_twin, 1: core_twin, 2: (core_twin + 2) % 4}[kind]
+        return pltpu.make_async_remote_copy(
+            src_ref=recv.at[c, pl.ds(1, 2)],
+            dst_ref=refreshed_ref.at[:, pl.ds(group_len * origin, group_len), c],
+            send_sem=fwd_send_sem.at[kind, c],
+            recv_sem=fwd_recv_sem.at[kind, c],
+            device_id=(x_twin if kind == 0 else core_twin, s),
+            device_id_type=MESH,
+        )
+
+    def keep(c):
+        return pltpu.make_async_copy(
+            recv.at[c, pl.ds(1, 2)],
+            refreshed_ref.at[:, pl.ds(group_len * p, group_len), c],
+            keep_sem.at[c],
+        )
+
+    def out_copy(c, step):
+        to = (s + step) % peers
+        return pltpu.make_async_remote_copy(
+            src_ref=out_send.at[c, pl.ds(rows * to, rows)],
+            dst_ref=attended_ref.at[:, s, c],
+            send_sem=out_send_sem.at[c, step],
+            recv_sem=out_recv_sem.at[c, step],
+            device_id=(p, to),
+            device_id_type=MESH,
+        )
+
+    def out_arrival(c, step):
+        origin = (s + peers - step) % peers
+        return pltpu.make_async_remote_copy(
+            src_ref=out_send.at[c, pl.ds(rows * origin, rows)],
+            dst_ref=attended_ref.at[:, origin, c],
+            send_sem=out_send_sem.at[c, step],
+            recv_sem=out_recv_sem.at[c, step],
+            device_id=(p, origin),
+            device_id_type=MESH,
+        )
+
+    def out_own(c):
+        return pltpu.make_async_copy(
+            out_send.at[c, pl.ds(rows * s, rows)], attended_ref.at[:, s, c], out_own_sem.at[c]
+        )
+
+    def follow(k):
+        for step in range(1, peers):
+            in_copy(k, step).wait_send()
+            if k + 2 < len(groups):
+                in_copy(k + 2, step).start()
+
+    for k in range(2):
+        for step in range(1, peers):
+            in_copy(k, step).start()
+
     counts_copy = pltpu.make_async_copy(counts_ref, counts, counts_sem.at[0])
     counts_copy.start()
     stale_copies = []
@@ -77,116 +176,6 @@
         )
         copy.start()
         own_copies.append(copy)
-    pl.semaphore_wait(barrier, peers + 1)
-
-    groups = [(0, 1, 2), (0, 0, 1)]
-    groups += [(c, 1, 2) for c in range(1, chunks)]
-    groups += [(c, 0, 1) for c in range(1, chunks)]
-
-    def in_copy(k, step):
-        c, first, count = groups[k]
-        to = (s + step) % peers
-        return pltpu.make_async_remote_copy(
-            src_ref=fresh_ref.at[pl.ds(first, count), :, to, c],
-            dst_ref=recv.at[c, pl.ds(first, count), pl.ds(rows * s, rows)],
-            send_sem=in_send_sem.at[k, step],
-            recv_sem=in_recv_sem.at[k, step],
-            device_id=(p, to),
-            device_id_type=MESH,
-        )
-
-    def in_arrival(k, step):
-        c, first, count = groups[k]
-        origin = (s + peers - step) % peers
-        return pltpu.make_async_remote_copy(
-            src_ref=fresh_ref.at[pl.ds(first, count), :, origin, c],
-            dst_ref=recv.at[c, pl.ds(first, count), pl.ds(rows * origin, rows)],
-            send_sem=in_send_sem.at[k, step],
-            recv_sem=in_recv_sem.at[k, step],
-            device_id=(p, origin),
-            device_id_type=MESH,
-        )
-
-    def forward(c, kind):
-        if kind == 2:
-            place = refreshed_ref.at[:, pl.ds(group_len * x_twin, group_len), c]
-            source = place
-        else:
-            place = refreshed_ref.at[:, pl.ds(group_len * p, group_len), c]
-            source = recv.at[c, pl.ds(1, 2)]
-        return pltpu.make_async_remote_copy(
-            src_ref=source,
-            dst_ref=place,
-            send_sem=fwd_send_sem.at[kind, c],
-            recv_sem=fwd_recv_sem.at[kind, c],
-            device_id=(x_twin if kind == 0 else core_twin, s),
-            device_id_type=MESH,
-        )
-
-    def forward_arrival(c, kind):
-        origin = {0: x_twin, 1: core_twin, 2: (core_twin + 2) % 4}[kind]
-        return pltpu.make_async_remote_copy(
-            src_ref=recv.at[c, pl.ds(1, 2)],
-            dst_ref=refreshed_ref.at[:, pl.ds(group_len * origin, group_len), c],
-            send_sem=fwd_send_sem.at[kind, c],
-            recv_sem=fwd_recv_sem.at[kind, c],
-            device_id=(x_twin if kind == 0 else core_twin, s),
-            device_id_type=MESH,
-        )
-
-    def keep(c):
-        return pltpu.make_async_copy(
-            recv.at[c, pl.ds(1, 2)],
-            refreshed_ref.at[:, pl.ds(group_len * p, group_len), c],
-            keep_sem.at[c],
-        )
-
-    def out_copy(c, step):
-        to = (s + step) % peers
-        return pltpu.make_async_remote_copy(
-            src_ref=out_send.at[c, pl.ds(rows * to, rows)],
-            dst_ref=attended_ref.at[:, s, c],
-            send_sem=out_send_sem.at[c, step],
-            recv_sem=out_recv_sem.at[c, step],
-            device_id=(p, to),
-            device_id_type=MESH,
-        )
-
-    def out_arrival(c, step):
-        origin = (s + peers - step) % peers
-        return pltpu.make_async_remote_copy(
-            src_ref=out_send.at[c, pl.ds(rows * origin, rows)],
-            dst_ref=attended_ref.at[:, origin, c],
-            send_sem=out_send_sem.at[c, step],
-            recv_sem=out_recv_sem.at[c, step],
-            device_id=(p, origin),
-            device_id_type=MESH,
-        )
-
-    def out_own(c):
-        return pltpu.make_async_copy(
-            out_send.at[c, pl.ds(rows * s, rows)], attended_ref.at[:, s, c], out_own_sem.at[c]
-        )
-
-    def follow(k):
-        for step in range(1, peers):
-            in_copy(k, step).wait_send()
-            if k + 2 < len(groups):
-                in_copy(k + 2, step).start()
-
-    for k in range(2):
-        for step in range(1, peers):
-            in_copy(k, step).start()
-
-    counts_copy.wait()
-    for copy in stale_copies:
-        copy.wait()
-    for c in range(chunks):
-        for which, target in ((0, keys), (1, values)):
-            wide[...] = stale_vmem[which, c].astype(jnp.float32).reshape(seq_len * tile, hdim)
-            for g in range(tile):
-                target[c * tile + g] = wide[pl.ds(g, seq_len, stride=tile), :].astype(jnp.bfloat16)
-
     masked_lanes = min(seq_len, -(-text_len // 128) * 128)
     position = lax.broadcasted_iota(jnp.int32, (1, masked_lanes), 1)
 
@@ -197,12 +186,19 @@
             part[pl.ds(g, group_len, stride=tile), :].astype(jnp.bfloat16) for g in range(tile)
         ]
 
-    def take_keys(c):
+    def send_keys(c):
         forward(c, 0).start()
         forward(c, 1).start()
         keep(c).start()
+
+    def store_keys(c):
         place = pl.ds(pl.multiple_of(group_len * p, 16), group_len)
         for which, target in ((1, keys), (2, values)):
+            stale_copies[2 * c + which - 1].wait()
+            block = stale_vmem[which - 1, c].astype(jnp.float32)
+            wide[...] = block.reshape(seq_len * tile, hdim)
+            for g in range(tile):
+                target[c * tile + g] = wide[pl.ds(g, seq_len, stride=tile), :].astype(jnp.bfloat16)
             for g, block in enumerate(rows_of_pairs(c, which)):
                 target[c * tile + g, place, :] = block
 
@@ -233,7 +229,11 @@
             out_copy(c, step).start()
         out_own(c).start()
 
-    relays = 0
+    def relay(c):
+        forward_arrival(c, 0).wait_recv()
+        forward(c, 2).start()
+
+    counts_copy.wait()
     for copy in own_copies:
         copy.wait()
     for k, (c, first, _) in enumerate(groups):
@@ -241,16 +241,15 @@
         for step in range(1, peers):
             in_arrival(k, step).wait_recv()
         if first == 1:
-            take_keys(c)
+            send_keys(c)
+            store_keys(c)
+            if c:
+                relay(c - 1)
         else:
             attend_chunk(c)
-        if k >= 2 and relays + 1 < chunks:
-            forward_arrival(relays, 0).wait_recv()
-            forward(relays, 2).start()
-            relays += 1
-
-    forward_arrival(chunks - 1, 0).wait_recv()
-    forward(chunks - 1, 2).start()
+            if c == max(chunks - 2, 0):
+                relay(chunks - 1)
+
     for c in range(chunks):
         for step in range(1, peers):
             out_copy(c, step).wait_send()

time: 89.6 us -> 89.7 us (level)
  no operation moved by 1% of the time
where the time goes in v6:
time: 89.7 us; the launch traced here: 89.6 us
  Pallas kernels  85.1 us (95%)
  local copies, waits for them, and re-layouts  3.88 us (4%)
    pallas_call x1, Pallas kernels, fused(): pl.pallas_call(functools.partial(fused_kernel, text_len), out_shape=(pltp...  85.1 us
    unnamed x2, local copies, waits for them, and re-layouts  3.88 us

profile of v6, /device:TPU:0, one launch (start us, length us, event | category | flops | bytes accessed | tf_op | source)
XLA Modules:
  0.0 89.6 jit_solution(2236942828450971912)
XLA Ops:
  0.6 85.1 %joint_attention.1 = (bf16[18,8,3,8,128]{4,3,2,1,0:T(8,128)(2,1)S(1)}, bf16[2,576,3,8,128]{4,3,2,1,0:T(8,128)(2,1)S(1)}) custom-call(s32[8]{0:T(128)} %counts_ref.1, bf16[3,18,8,3,8,128]{5,4,3,2,1,0:T(8,128)(2,1)} %bitcast.7, bf16[2,576,3,8,128]{4,3,2,1,0:T(8,128)(2,1)} %bitcast.6), custom_call_target="tpu_custom_call" | custom-call | tf_op jit(solution)/shard_map/joint_attention/pallas_call | solution.py:279
  85.7 0.9 %copy.7 = bf16[18,192,128]{2,1,0:T(8,128)(2,1)} copy(bf16[18,192,128]{2,1,0:T(8,128)(2,1)S(1)} %bitcast.5) | data formatting | bytes 1769472
  86.6 3.0 %copy.8 = bf16[2,576,24,128]{3,2,1,0:T(8,128)(2,1)} copy(bf16[2,576,24,128]{3,2,1,0:T(8,128)(2,1)S(1)} %bitcast.4) | data formatting | bytes 14155776
